TPU v7x, 32 devices: a whole 2x2x4 slice. The times are simulated.
32 devices in a mesh: dp: 4 (over z), tx: 2 (over core), ty: 4 (over y, x).
Axes of the slice: x: 2, y: 2, z: 4, core: 2. Of those that a mesh axis runs over, the one named last changes fastest.
Arguments:
- tokens: bfloat16 [2048, 2048], P('dp', 'tx'), may hold values from -6 to 6
- query_weight: bfloat16 [2048, 4, 512], P(None, 'ty', 'tx'), may hold values from -0.25 to 0.25
- key_value_weight: bfloat16 [2048, 4, 128], P(None, 'ty'), may hold values from -0.125 to 0.125
- output_weight: bfloat16 [4, 512, 2048], P('ty', 'tx'), may hold values from -0.5 to 0.5
- cache: bfloat16 [4, 4, 2048, 128], P('dp', 'ty'), may hold values from -300 to 300
- lengths: int32 [4], replicated, may hold values from 0 to 8192, as said below
- offsets: int32 [4], replicated, may hold values from 0 to 2047
- slots: int32 [4], replicated, may hold values from 0 to 3, each once
Outputs:
- mixed: bfloat16 [2048, 2048], P('dp', ('tx', 'ty'))
- new_cache: bfloat16 [4, 4, 2048, 128], P('dp', 'ty')
Inputs may be any that keep to these rules, and one draw needn't show every extreme that they name: `lengths`: some request has exactly 8192 cached positions. `slots`: every slot belongs to exactly one request.
All inputs are finite; a program needn't handle non-finite values.
Results may differ from a plain program's by a relative error of at most 0.012.
The roundings to bfloat16 on the way count: a program that leaves them out, or rounds other values in their place, can miss the bound.
Values may be sent and summed in bfloat16 or wider, within the bound.
A program may use at most 64 MiB of HBM per device.

v0:
```python
import math

import jax
import jax.numpy as jnp
from jax import lax
from jax.sharding import PartitionSpec as P

HEAD_SIZE = 64
WINDOW_LENGTH = 2048


EPS = 1e-05


def apply_rotary(values, token_positions):
    width = values.shape[-1]
    half_width = width // 2
    freqs = jnp.exp(jnp.arange(half_width, dtype=jnp.float32) * (-2.0 * math.log(10000.0) / width))
    angles = token_positions.astype(jnp.float32)[:, None] * freqs[None, :]
    cosine = jnp.cos(angles)[:, None, :]
    sine = jnp.sin(angles)[:, None, :]
    leading = values[..., :half_width]
    trailing = values[..., half_width:]
    return jnp.concatenate(
        [leading * cosine - trailing * sine, trailing * cosine + leading * sine], axis=-1
    )


def carry_in(window):
    return lax.all_to_all(window, "dp", split_axis=0, concat_axis=0, tiled=True)


def carry_out(window):
    return lax.all_to_all(window, "dp", split_axis=0, concat_axis=0, tiled=True)


def reorder(window, order, groups):
    columns = window.shape[1]
    blocks = window.reshape(groups, window.shape[0] // groups, columns)
    return jnp.take(blocks, order, axis=0).reshape(window.shape[0], columns)


def per_device(
    tokens, query_weight, key_value_weight, output_weight, cache, lengths, offsets, slots
):
    request = lax.axis_index("dp")
    groups = lax.axis_size("dp")
    whole = lax.all_gather(tokens, "tx", axis=1, tiled=True)
    rows_new = whole.shape[0]
    width = whole.shape[1]
    floats = whole.astype(jnp.float32)
    normalized_input = (
        floats * lax.rsqrt(jnp.mean(floats * floats, axis=1, keepdims=True) + EPS)
    ).astype(jnp.bfloat16)
    owners = jnp.arange(slots.shape[0], dtype=jnp.int32)
    inverse = jnp.sum(jnp.where(slots[None, :] == owners[:, None], owners[None, :], 0), axis=1)
    spread_in = carry_in(cache[0, 0])
    window = carry_in(reorder(spread_in, slots, groups))
    query_cols = query_weight.shape[2]
    heads = query_cols // HEAD_SIZE
    queries = jnp.dot(
        normalized_input,
        query_weight.reshape(width, query_cols),
        preferred_element_type=jnp.float32,
    )
    rotation_pairs = jnp.dot(
        normalized_input,
        key_value_weight.reshape(width, 2 * HEAD_SIZE),
        preferred_element_type=jnp.float32,
    )
    length = lengths[request]
    offset = offsets[request]
    token_positions = length + jnp.arange(rows_new, dtype=jnp.int32)
    query_rotated = apply_rotary(
        queries.reshape(rows_new, heads, HEAD_SIZE), token_positions
    ).astype(jnp.bfloat16)
    new_keys = apply_rotary(rotation_pairs[:, None, :HEAD_SIZE], token_positions)[:, 0].astype(
        jnp.bfloat16
    )
    new_values = rotation_pairs[:, HEAD_SIZE:].astype(jnp.bfloat16)
    factor = 1.0 / math.sqrt(HEAD_SIZE)
    rows = jnp.arange(rows_new, dtype=jnp.int32)
    new_mask = rows[None, :] <= rows[:, None]
    cycle = jnp.arange(WINDOW_LENGTH, dtype=jnp.int32)
    held = length - 1 - jnp.mod(offset - 1 - cycle, WINDOW_LENGTH)
    cache_mask = (held[None, :] >= 0) & (held[None, :] > token_positions[:, None] - WINDOW_LENGTH)
    mask_all = jnp.concatenate([cache_mask, new_mask], axis=1)
    keys_all = jnp.concatenate([window[:, :HEAD_SIZE], new_keys], axis=0)
    values_all = jnp.concatenate([window[:, HEAD_SIZE:], new_values], axis=0)

    def one_head(query_rows):
        scores = (
            jnp.einsum("qd,kd->qk", query_rows, keys_all, preferred_element_type=jnp.float32)
            * factor
        )
        scores = jnp.where(mask_all, scores, -jnp.inf)
        top = jnp.max(scores, axis=1, keepdims=True)
        powers = jnp.exp(scores - top)
        total = jnp.sum(powers, axis=1, keepdims=True)
        weights = powers.astype(jnp.bfloat16)
        summed = jnp.dot(weights, values_all, preferred_element_type=jnp.float32)
        return (summed / total).astype(jnp.bfloat16)

    outputs = lax.map(one_head, jnp.transpose(query_rotated, (1, 0, 2)))
    attended = jnp.transpose(outputs, (1, 0, 2)).reshape(rows_new, heads * HEAD_SIZE)
    rolled = jnp.roll(window, -offset, axis=0)
    entry = jnp.concatenate([new_keys, new_values], axis=1)
    updated = jnp.roll(jnp.concatenate([entry, rolled[rows_new:]], axis=0), offset, axis=0)
    spread_out = carry_out(updated)
    returned = carry_out(reorder(spread_out, inverse, groups))
    new_cache = returned[None, None]
    out_rows = output_weight.reshape(output_weight.shape[1], width)
    partial_value = jnp.dot(attended, out_rows, preferred_element_type=jnp.float32)
    summed_out = lax.psum_scatter(partial_value, ("tx", "ty"), scatter_dimension=1, tiled=True)
    mixed = summed_out.astype(jnp.bfloat16)
    return (mixed, new_cache)


def solution(mesh):
    return jax.shard_map(
        per_device,
        mesh=mesh,
        in_specs=(
            P("dp", "tx"),
            P(None, "ty", "tx"),
            P(None, "ty", None),
            P("ty", "tx", None),
            P("dp", "ty", None, None),
            P(),
            P(),
            P(),
        ),
        out_specs=(P("dp", ("tx", "ty")), P("dp", "ty", None, None)),
        check_vma=False,
    )
```

profile of v0, /device:TPU:0, one launch (start us, length us, event | category | flops | bytes accessed | tf_op | source)
XLA Modules:
  0.0 143.7 jit_solution(1848442836865491196)
XLA Ops:
  7.2 0.0 copy-start
  7.2 0.0 copy-start.8
  7.2 0.0 all-gather.2.cloned.1.call-start
  7.2 0.7 all-gather.2.cloned.1.call-update
  7.9 6.3 %all-to-all-start = ((bf16[4,512,128]{2,1,0:T(8,128)(2,1)}), bf16[4,512,128]{2,1,0:T(8,128)(2,1)S(1)}, u32[]{:S(2)}, u32[]{:S(2)}) async-start(bf16[4,512,128]{2,1,0:T(8,128)(2,1)} %bitcast.56), calls=%async_computation | async-start | bytes 1048576 | tf_op jit(solution)/shard_map/all_to_all | solution.py:30
  14.3 1.2 dynamic_slice.13
  15.5 0.6 fusion.48
  16.1 0.7 fusion.47
  16.8 1.3 dynamic_slice.14
  19.4 0.7 compare_select_fusion.1
  20.1 0.1 iota_compare_fusion
  20.2 2.3 %copy.20 = bf16[2048,1,256]{0,2,1:T(8,128)(2,1)} copy(bf16[2048,1,256]{2,0,1:T(8,128)(2,1)} %param.15) | data formatting | bytes 2097152 | tf_op args[1]
  22.5 0.3 multiply_cosine_fusion.1
  22.8 5.9 %all-to-all-done = bf16[4,512,128]{2,1,0:T(8,128)(2,1)S(1)} async-done(((bf16[4,512,128]{2,1,0:T(8,128)(2,1)}), bf16[4,512,128]{2,1,0:T(8,128)(2,1)S(1)}, u32[]{:S(2)}, u32[]{:S(2)}) %all-to-all-start) | async-done | bytes 524320 | tf_op jit(solution)/shard_map/all_to_all | solution.py:30
  28.7 0.6 gather_fusion
  29.4 0.9 broadcast_select_fusion.1
  30.3 3.5 %all-to-all-start.1 = ((bf16[4,512,128]{2,1,0:T(8,128)(2,1)}), bf16[4,512,128]{2,1,0:T(8,128)(2,1)S(1)}, u32[]{:S(2)}, u32[]{:S(2)}) async-start(bf16[4,512,128]{2,1,0:T(8,128)(2,1)} %broadcast_select_fusion.1), calls=%async_computation.1 | async-start | bytes 1048576 | tf_op jit(solution)/shard_map/all_to_all | solution.py:30
  33.8 0.0 reduce-scatter.2.cloned.1.call-start
  33.8 0.7 compare_and_fusion
  34.6 0.1 pad_add_fusion
  34.7 13.1 %all-to-all-done.1 = bf16[4,512,128]{2,1,0:T(8,128)(2,1)S(1)} async-done(((bf16[4,512,128]{2,1,0:T(8,128)(2,1)}), bf16[4,512,128]{2,1,0:T(8,128)(2,1)S(1)}, u32[]{:S(2)}, u32[]{:S(2)}) %all-to-all-start.1) | async-done | bytes 524320 | tf_op jit(solution)/shard_map/all_to_all | solution.py:30
  47.8 1.1 fusion.50
  48.9 2.1 %fusion.20 = f32[512]{0:T(512)S(1)} fusion(bf16[512,2048]{1,0:T(8,128)(2,1)} %all-gather.2.cloned.1.call-done), kind=kLoop, calls=%fused_computation.18 | loop fusion | flops 3145216 | bytes 2099200 | tf_op jit(solution)/shard_map/reduce_sum | solution.py:53
  51.0 2.6 %fusion.26 = f32[512,128]{0,1:T(8,128)S(1)} fusion(bf16[512,2048]{1,0:T(8,128)(2,1)} %all-gather.2.cloned.1.call-done, f32[512]{0:T(512)S(1)} %add_rsqrt_fusion, bf16[2048,1,128]{2,0,1:T(8,128)(2,1)} %param.16), kind=kOutput, calls=%fused_computation.32 | convolution fusion | flops 271581184 | bytes 2885632 | tf_op jit(solution)/shard_map/dot_general | solution.py:66
  53.6 0.3 fusion.39
  54.0 0.7 copy.21
  54.7 0.8 copy.22
  55.5 2.7 %fusion.22 = f32[512,4,64]{0,2,1:T(8,128)S(1)} fusion(bf16[4,64,2048]{2,1,0:T(8,128)(2,1)} %bitcast.54, bf16[512,2048]{1,0:T(8,128)(2,1)} %all-gather.2.cloned.1.call-done, f32[512]{0:T(512)S(1)} %add_rsqrt_fusion), kind=kOutput, calls=%fused_computation.21 | convolution fusion | flops 540016640 | bytes 3672064 | tf_op jit(solution)/shard_map/dot_general | solution.py:61
  58.2 0.1 subtract_convert_fusion
  58.3 0.7 maximum_bitcast_fusion
  59.0 0.0 copy-done.7
  59.0 2.3 %pad_maximum_fusion = (bf16[2560,64]{1,0:T(8,128)(2,1)S(1)}, bf16[2560,64]{1,0:T(8,128)(2,1)}) fusion(bf16[512,64]{1,0:T(8,128)(2,1)S(1)} %copy-done.6, bf16[2048,64]{1,0:T(8,128)(2,1)} %get-tuple-element.72, bf16[512,64]{1,0:T(8,128)(2,1)S(1)} %copy-done.7, bf16[2048,64]{1,0:T(8,128)(2,1)} %get-tuple-element.71), kind=kLoop, calls=%fused_computation.33 | loop fusion | flops 1310720 | bytes 1310720 | tf_op jit(solution)/shard_map/concatenate | solution.py:88
  61.3 18.8 %while.10 = (s32[]{:T(128)}, bf16[4,512,64]{1,2,0:T(8,128)(2,1)}, bf16[4,512,64]{1,2,0:T(8,128)(2,1)}, bf16[2560,64]{1,0:T(8,128)(2,1)S(1)}, pred[512,2560]{1,0:...) while((s32[]{:T(128)}, bf16[4,512,64]{1,2,0:T(8,128)(2,1)}, bf16[4,512,64]{1,2,0:T(8,128)(2,1)}, ...), condition=%wide.region_4.6_spmd, body=%wide.region_1.5_spmd.sunk | while | flops 344783872 | bytes 19146872 | solution.py:104
  61.3 2.0 %fusion.64 = (f32[512]{0:T(512)S(1)}, f32[512,2560]{1,0:T(8,128)S(1)}) fusion(pred[512,2560]{1,0:T(32,128)(4,1)S(1)} %get-tuple-element.138, bf16[2560,64]{1,0:T(8,128)(2,1)S(1)} %get-tuple-element.137, bf16[4,512,64]{1,2,0:T(8,128)(2,1)} %get-tuple-element.136, s32[]{:T(128)S(6)} %copy.29), kind=kOutput, calls=%fused_computation.83.clone.1 | convolution fusion | flops 171703808 | bytes 6948868 | tf_op jit(solution)/shard_map/while/body/eval_jaxpr/qd,kd->qk/dot_general | solution.py:93
  63.3 0.8 fusion.65
  64.2 0.2 copy-done.1
  64.4 1.6 %fusion.66 = bf16[4,512,64]{1,2,0:T(8,128)(2,1)} fusion(bf16[4,512,64]{1,2,0:T(8,128)(2,1)} %get-tuple-element.128, s32[]{:T(128)S(6)} %copy.29, bf16[2560,64]{1,0:T(8,128)(2,1)S(1)} %copy-done.1, f32[512,2560]{1,0:T(8,128)S(1)} %get-tuple-element.118, f32[512]{0:T(512)S(1)} %get-tuple-element.119, f32[512]{0:T(512)S(1)} %fusion.65), kind=kOutput, calls=%fused_computation.11.clone.1 | convolution fusion | flops 170459136 | bytes 5640196 | tf_op jit(solution)/shard_map/while/body/eval_jaxpr/dot_general | solution.py:101
  66.0 2.0 %fusion.64 = (f32[512]{0:T(512)S(1)}, f32[512,2560]{1,0:T(8,128)S(1)}) fusion(pred[512,2560]{1,0:T(32,128)(4,1)S(1)} %get-tuple-element.138, bf16[2560,64]{1,0:T(8,128)(2,1)S(1)} %get-tuple-element.137, bf16[4,512,64]{1,2,0:T(8,128)(2,1)} %get-tuple-element.136, s32[]{:T(128)S(6)} %copy.29), kind=kOutput, calls=%fused_computation.83.clone.1 | convolution fusion | flops 171703808 | bytes 6948868 | tf_op jit(solution)/shard_map/while/body/eval_jaxpr/qd,kd->qk/dot_general | solution.py:93
  68.0 0.8 fusion.65
  68.9 0.2 copy-done.1
  69.1 1.6 %fusion.66 = bf16[4,512,64]{1,2,0:T(8,128)(2,1)} fusion(bf16[4,512,64]{1,2,0:T(8,128)(2,1)} %get-tuple-element.128, s32[]{:T(128)S(6)} %copy.29, bf16[2560,64]{1,0:T(8,128)(2,1)S(1)} %copy-done.1, f32[512,2560]{1,0:T(8,128)S(1)} %get-tuple-element.118, f32[512]{0:T(512)S(1)} %get-tuple-element.119, f32[512]{0:T(512)S(1)} %fusion.65), kind=kOutput, calls=%fused_computation.11.clone.1 | convolution fusion | flops 170459136 | bytes 5640196 | tf_op jit(solution)/shard_map/while/body/eval_jaxpr/dot_general | solution.py:101
  70.7 2.0 %fusion.64 = (f32[512]{0:T(512)S(1)}, f32[512,2560]{1,0:T(8,128)S(1)}) fusion(pred[512,2560]{1,0:T(32,128)(4,1)S(1)} %get-tuple-element.138, bf16[2560,64]{1,0:T(8,128)(2,1)S(1)} %get-tuple-element.137, bf16[4,512,64]{1,2,0:T(8,128)(2,1)} %get-tuple-element.136, s32[]{:T(128)S(6)} %copy.29), kind=kOutput, calls=%fused_computation.83.clone.1 | convolution fusion | flops 171703808 | bytes 6948868 | tf_op jit(solution)/shard_map/while/body/eval_jaxpr/qd,kd->qk/dot_general | solution.py:93
  72.7 0.8 fusion.65
  73.5 0.2 copy-done.1
  73.8 1.6 %fusion.66 = bf16[4,512,64]{1,2,0:T(8,128)(2,1)} fusion(bf16[4,512,64]{1,2,0:T(8,128)(2,1)} %get-tuple-element.128, s32[]{:T(128)S(6)} %copy.29, bf16[2560,64]{1,0:T(8,128)(2,1)S(1)} %copy-done.1, f32[512,2560]{1,0:T(8,128)S(1)} %get-tuple-element.118, f32[512]{0:T(512)S(1)} %get-tuple-element.119, f32[512]{0:T(512)S(1)} %fusion.65), kind=kOutput, calls=%fused_computation.11.clone.1 | convolution fusion | flops 170459136 | bytes 5640196 | tf_op jit(solution)/shard_map/while/body/eval_jaxpr/dot_general | solution.py:101
  75.4 2.0 %fusion.64 = (f32[512]{0:T(512)S(1)}, f32[512,2560]{1,0:T(8,128)S(1)}) fusion(pred[512,2560]{1,0:T(32,128)(4,1)S(1)} %get-tuple-element.138, bf16[2560,64]{1,0:T(8,128)(2,1)S(1)} %get-tuple-element.137, bf16[4,512,64]{1,2,0:T(8,128)(2,1)} %get-tuple-element.136, s32[]{:T(128)S(6)} %copy.29), kind=kOutput, calls=%fused_computation.83.clone.1 | convolution fusion | flops 171703808 | bytes 6948868 | tf_op jit(solution)/shard_map/while/body/eval_jaxpr/qd,kd->qk/dot_general | solution.py:93
  77.4 0.8 fusion.65
  78.2 0.2 copy-done.1
  78.5 1.6 %fusion.66 = bf16[4,512,64]{1,2,0:T(8,128)(2,1)} fusion(bf16[4,512,64]{1,2,0:T(8,128)(2,1)} %get-tuple-element.128, s32[]{:T(128)S(6)} %copy.29, bf16[2560,64]{1,0:T(8,128)(2,1)S(1)} %copy-done.1, f32[512,2560]{1,0:T(8,128)S(1)} %get-tuple-element.118, f32[512]{0:T(512)S(1)} %get-tuple-element.119, f32[512]{0:T(512)S(1)} %fusion.65), kind=kOutput, calls=%fused_computation.11.clone.1 | convolution fusion | flops 170459136 | bytes 5640196 | tf_op jit(solution)/shard_map/while/body/eval_jaxpr/dot_general | solution.py:101
  80.1 0.0 copy-done
  80.1 3.6 %fusion.24 = f32[512,2048]{1,0:T(8,128)} fusion(bf16[512,256]{0,1:T(8,128)(2,1)} %bitcast.55, bf16[1,256,2048]{2,1,0:T(8,128)(2,1)S(1)} %copy-done), kind=kOutput, calls=%fused_computation.29 | convolution fusion | flops 536870912 | bytes 5505024 | tf_op jit(solution)/shard_map/dot_general | solution.py:113
  83.7 0.0 reduce-scatter.2.cloned.1.call-update
  86.3 1.5 %fusion.33 = bf16[1536,128]{1,0:T(8,128)(2,1)S(1)} fusion(s32[]{:T(128)S(6)} %add.89, bf16[2048,128]{1,0:T(8,128)(2,1)S(1)} %bitcast.52), kind=kLoop, calls=%fused_computation.41 | loop fusion | flops 786432 | bytes 917508 | tf_op jit(solution)/shard_map/jit(_roll_dynamic)/concatenate | solution.py:106
  87.9 0.1 copy.24
  88.0 4.1 %fusion.30 = bf16[2048,128]{1,0:T(8,128)(2,1)} fusion(s32[]{:T(128)S(6)} %select_n.54, bf16[512,128]{1,0:T(8,128)(2,1)S(1)} %copy.24, bf16[1536,128]{1,0:T(8,128)(2,1)S(1)} %fusion.33), kind=kLoop, calls=%fused_computation.36 | loop fusion | flops 2097152 | bytes 1048580 | tf_op jit(solution)/shard_map/jit(_roll_dynamic)/concatenate | solution.py:108
  92.1 3.5 %all-to-all-start.2 = ((bf16[4,512,128]{2,1,0:T(8,128)(2,1)}), bf16[4,512,128]{2,1,0:T(8,128)(2,1)S(1)}, u32[]{:S(2)}, u32[]{:S(2)}) async-start(bf16[4,512,128]{2,1,0:T(8,128)(2,1)} %bitcast.17), calls=%async_computation.3 | async-start | bytes 1048576 | tf_op jit(solution)/shard_map/all_to_all | solution.py:34
  95.6 0.1 select_reduce_fusion
  95.8 13.8 %all-to-all-done.2 = bf16[4,512,128]{2,1,0:T(8,128)(2,1)S(1)} async-done(((bf16[4,512,128]{2,1,0:T(8,128)(2,1)}), bf16[4,512,128]{2,1,0:T(8,128)(2,1)S(1)}, u32[]{:S(2)}, u32[]{:S(2)}) %all-to-all-start.2) | async-done | bytes 524320 | tf_op jit(solution)/shard_map/all_to_all | solution.py:34
  109.6 0.6 gather_fusion.1
  110.2 0.1 broadcast_select_fusion
  110.4 16.4 %all_to_all.33 = bf16[4,512,128]{2,1,0:T(8,128)(2,1)S(1)} all-to-all(bf16[4,512,128]{2,1,0:T(8,128)(2,1)S(1)} %broadcast_select_fusion), channel_id=1, replica_groups=mesh['dp'=4,'tx'=2,'ty'=4] {'dp'}, dimensions={0} | all-to-all | bytes 1048576 | tf_op jit(solution)/shard_map/all_to_all | solution.py:34
  126.7 7.6 %reduce-scatter.2.cloned.1.call-done = f32[512,256]{1,0:T(8,128)} async-done(((f32[512,2048]{1,0:T(8,128)}), f32[512,256]{1,0:T(8,128)}) %reduce-scatter.2.cloned.1.call-update) | async-done | bytes 524304 | tf_op jit(solution)/shard_map/reduce_scatter | solution.py:114
  134.3 1.8 %convert_element_type.33 = bf16[512,256]{1,0:T(8,128)(2,1)} convert(f32[512,256]{1,0:T(8,128)} %reduce-scatter.2.cloned.1.call-done) | non-fusion elementwise | flops 131072 | bytes 786432 | tf_op jit(solution)/shard_map/convert_element_type | solution.py:115
  136.1 0.8 copy.40
  (31 shorter events, 0.2 us)
Async XLA Ops:
  7.2 72.9 %copy-start = (bf16[1,256,2048]{2,1,0:T(8,128)(2,1)S(1)}, bf16[1,256,2048]{2,1,0:T(8,128)(2,1)}, u32[]{:S(2)}) copy-start(bf16[1,256,2048]{2,1,0:T(8,128)(2,1)} %param.17) | copy-start | bytes 3145732
  7.2 15.3 %copy-start.8 = (s32[4]{0:T(128)S(1)}, s32[4]{0:T(128)}, u32[]{:S(2)}) copy-start(s32[4]{0:T(128)} %param.21) | copy-start | bytes 52
  7.2 41.7 %all-gather.2.cloned.1.call-start = ((), (), s32[]{:S(2)}) async-start(), calls=%async_computation.5 | async-start | bytes 3145728 | tf_op jit(solution)/shard_map/all_gather | solution.py:48
  7.9 20.8 %all-to-all-start = ((bf16[4,512,128]{2,1,0:T(8,128)(2,1)}), bf16[4,512,128]{2,1,0:T(8,128)(2,1)S(1)}, u32[]{:S(2)}, u32[]{:S(2)}) async-start(bf16[4,512,128]{2,1,0:T(8,128)(2,1)} %bitcast.56), calls=%async_computation | async-start | bytes 1048576 | tf_op jit(solution)/shard_map/all_to_all | solution.py:30
  30.3 17.4 %all-to-all-start.1 = ((bf16[4,512,128]{2,1,0:T(8,128)(2,1)}), bf16[4,512,128]{2,1,0:T(8,128)(2,1)S(1)}, u32[]{:S(2)}, u32[]{:S(2)}) async-start(bf16[4,512,128]{2,1,0:T(8,128)(2,1)} %broadcast_select_fusion.1), calls=%async_computation.1 | async-start | bytes 1048576 | tf_op jit(solution)/shard_map/all_to_all | solution.py:30
  33.8 100.6 %reduce-scatter.2.cloned.1.call-start = ((), (), s32[]{:S(2)}) async-start(), calls=%async_computation.6 | async-start | bytes 4718592 | tf_op jit(solution)/shard_map/reduce_scatter | solution.py:114
  53.6 5.4 %copy-start.2 = (bf16[512,64]{0,1:T(8,128)(2,1)}, bf16[512,64]{0,1:T(8,128)(2,1)S(1)}, u32[]{:S(2)}) copy-start(bf16[512,64]{0,1:T(8,128)(2,1)S(1)} %slice.59) | copy-start | bytes 196612
  54.0 5.1 %copy-start.4 = (bf16[512,64]{0,1:T(8,128)(2,1)}, bf16[512,64]{0,1:T(8,128)(2,1)S(1)}, u32[]{:S(2)}) copy-start(bf16[512,64]{0,1:T(8,128)(2,1)S(1)} %maximum_bitcast_fusion.1) | copy-start | bytes 196612
  55.5 3.5 %copy-start.6 = (bf16[512,64]{1,0:T(8,128)(2,1)S(1)}, bf16[512,64]{1,0:T(8,128)(2,1)}, u32[]{:S(2)}) copy-start(bf16[512,64]{1,0:T(8,128)(2,1)} %copy.21) | copy-start | bytes 196612
  55.5 3.5 %copy-start.7 = (bf16[512,64]{1,0:T(8,128)(2,1)S(1)}, bf16[512,64]{1,0:T(8,128)(2,1)}, u32[]{:S(2)}) copy-start(bf16[512,64]{1,0:T(8,128)(2,1)} %copy.22) | copy-start | bytes 196612
  63.3 1.1 copy-start.1
  68.0 1.1 copy-start.1
  72.7 1.1 copy-start.1
  77.4 1.1 copy-start.1
  83.7 4.1 %copy-start.3 = (bf16[512,64]{0,1:T(8,128)(2,1)S(1)}, bf16[512,64]{0,1:T(8,128)(2,1)}, u32[]{:S(2)}) copy-start(bf16[512,64]{0,1:T(8,128)(2,1)} %copy-done.2) | copy-start | bytes 196612
  83.7 4.1 %copy-start.5 = (bf16[512,64]{0,1:T(8,128)(2,1)S(1)}, bf16[512,64]{0,1:T(8,128)(2,1)}, u32[]{:S(2)}) copy-start(bf16[512,64]{0,1:T(8,128)(2,1)} %copy-done.4) | copy-start | bytes 196612
  92.1 17.4 %all-to-all-start.2 = ((bf16[4,512,128]{2,1,0:T(8,128)(2,1)}), bf16[4,512,128]{2,1,0:T(8,128)(2,1)S(1)}, u32[]{:S(2)}, u32[]{:S(2)}) async-start(bf16[4,512,128]{2,1,0:T(8,128)(2,1)} %bitcast.17), calls=%async_computation.3 | async-start | bytes 1048576 | tf_op jit(solution)/shard_map/all_to_all | solution.py:34
Sparse Core Ops, SparseCore 0:
  9.6 13.2 all-gather.1
  83.9 50.4 reduce-scatter.1
where the time goes:
time: 145 us; the launch traced here: 144 us
  waiting for transfers between devices  41.1 us (28%)
  matrix products  23.3 us (16%)
  other arithmetic  20.7 us (14%)
  between operations  18.1 us (12%)
  blocking collectives  16.4 us (11%)
  starting transfers between devices  13.4 us (9%)
  local copies, waits for them, and re-layouts  10.8 us (7%)
    all_to_all x2, waiting for transfers between devices, carry_in(): return lax.all_to_all(window, 'dp', split_axis=0, concat_axis=0, tiled=True)  19 us
    all_to_all x1, blocking collectives, carry_out(): return lax.all_to_all(window, 'dp', split_axis=0, concat_axis=0, tiled=True)  16.4 us
    all_to_all x1, waiting for transfers between devices, carry_out(): return lax.all_to_all(window, 'dp', split_axis=0, concat_axis=0, tiled=True)  13.8 us
    all_to_all x2, starting transfers between devices, carry_in(): return lax.all_to_all(window, 'dp', split_axis=0, concat_axis=0, tiled=True)  9.8 us
    dot_general x4, matrix products, one_head(): jnp.einsum('qd,kd->qk', query_rows, keys_all, preferred_element_type=jnp....  7.91 us
    reduce_scatter x1, waiting for transfers between devices, per_device(): lax.psum_scatter(partial_value, ('tx', 'ty'), scatter_dimension=1, tiled=...  7.61 us
    dot_general x4, matrix products, one_head(): summed = jnp.dot(weights, values_all, preferred_element_type=jnp.float32)  6.48 us
    concatenate x1, other arithmetic, per_device(): jnp.roll(jnp.concatenate([entry, rolled[rows_new:]], axis=0), offset, axi...  4.14 us
  transfers between devices with their start and end apart: 5, of which 4 were waited for; matrix products, arithmetic and copies ran while one was open for 12% of the time, Pallas kernels for 0%

commit v1 on v0

v1 whole, which is shorter than its diff:
```python
import functools
import math

import jax
import jax.numpy as jnp
from jax import lax
from jax.experimental import pallas as pl
from jax.experimental.pallas import tpu as pltpu
from jax.sharding import PartitionSpec as P

HEAD_SIZE = 64
WINDOW_LENGTH = 2048
EPS = 1e-05
LANES = 128
ROW_BLOCK = 128
PROJECT_ROWS = 256
KEY_CHUNK = 512
MESH = pl.DeviceIdType.MESH


def remote(src, dst, send_sem, recv_sem, device):
    return pltpu.make_async_remote_copy(
        src_ref=src, dst_ref=dst, send_sem=send_sem, recv_sem=recv_sem, device_id=device, device_id_type=MESH
    )


def contract_last(left, right):
    return lax.dot_general(left, right, (((1,), (1,)), ((), ())), preferred_element_type=jnp.float32)


def matmul(left, right):
    return jnp.dot(left, right, preferred_element_type=jnp.float32)


def kernel(
    zn, yn,
    tokens, query_weight, key_value_weight, output_weight, cache, cosine, sine, lengths, offsets, slots,
    mixed, new_cache,
    tok, qw, kvw, old, wbuf, spread, stage, kv, ents, qs, att, score, mine, psend, precv,
    local_sem, tok_sem, w_send, w_recv, s_send, s_recv, g_send, g_recv, half_sem, e_send, e_recv,
    a_send, a_recv, p_send, p_recv,
):
    me = lax.axis_index("dp")
    tx = lax.axis_index("tx")
    ty = lax.axis_index("ty")
    rows = tok.shape[1]
    half_width = tok.shape[2]
    cols = mixed.shape[1]
    heads = qs.shape[0]
    piece = spread.shape[1]
    half_rows = zn * piece
    blocks = rows // ROW_BLOCK
    sibling = {"tx": 1 - tx}

    def z_peer(d):
        return lax.rem(me + d, zn)

    def y_peer(d):
        return lax.rem(ty + d, yn)

    local = [
        pltpu.make_async_copy(tokens, tok.at[tx], local_sem.at[0]),
        pltpu.make_async_copy(query_weight, qw, local_sem.at[1]),
        pltpu.make_async_copy(key_value_weight, kvw, local_sem.at[2]),
        pltpu.make_async_copy(cache.at[0, 0], old, local_sem.at[3]),
        pltpu.make_async_copy(
            cache.at[0, 0, pl.ds(pl.multiple_of((tx * zn + me) * piece, piece), piece)],
            spread.at[0], local_sem.at[4],
        ),
    ]

    def w_columns(side, block):
        core = tx if side == 0 else 1 - tx
        return output_weight.at[0, :, pl.ds(pl.multiple_of((core * yn + block) * cols, cols), cols)]

    for side in range(2):
        local.append(pltpu.make_async_copy(w_columns(side, ty), wbuf.at[0, side], local_sem.at[5 + side]))
    for copy in local:
        copy.start()

    barrier = pltpu.get_barrier_semaphore()
    for d in range(1, zn):
        pl.semaphore_signal(barrier, inc=1, device_id={"dp": z_peer(d)}, device_id_type=MESH)
    for d in range(1, yn):
        pl.semaphore_signal(barrier, inc=1, device_id={"ty": y_peer(d)}, device_id_type=MESH)
    pl.semaphore_signal(barrier, inc=1, device_id=sibling, device_id_type=MESH)
    pl.semaphore_wait(barrier, zn + yn - 1)

    tok_copy = remote(tokens, tok.at[tx], tok_sem.at[0], tok_sem.at[1], sibling)
    tok_copy.start()
    spread_copies = []
    for d in range(1, zn):
        source = cache.at[0, 0, pl.ds(pl.multiple_of((tx * zn + z_peer(d)) * piece, piece), piece)]
        spread_copies.append(
            remote(source, spread.at[d], s_send.at[d], s_recv.at[d], {"dp": z_peer(d)})
        )
        spread_copies[-1].start()
    w_copies = []
    for d in range(1, yn):
        for side in range(2):
            w_copies.append(
                remote(
                    w_columns(side, y_peer(d)), wbuf.at[d, side], w_send.at[d, side], w_recv.at[d, side],
                    {"ty": y_peer(d)},
                )
            )
            w_copies[-1].start()

    length = lengths[me]
    offset = offsets[me]
    lane = lax.broadcasted_iota(jnp.int32, (PROJECT_ROWS, LANES), 1)
    first_half = lax.rem(lane, HEAD_SIZE) < HEAD_SIZE // 2
    key_lane = lane < HEAD_SIZE

    def project(step):
        at = pl.ds(step * PROJECT_ROWS, PROJECT_ROWS)
        left = tok[0, at, :].astype(jnp.float32)
        right = tok[1, at, :].astype(jnp.float32)
        squares = jnp.sum(left * left + right * right, axis=1, keepdims=True)
        scale = lax.rsqrt(squares * (1.0 / (2 * half_width)) + EPS)
        left = (left * scale).astype(jnp.bfloat16)
        right = (right * scale).astype(jnp.bfloat16)
        queries = matmul(left, qw[:half_width, :]) + matmul(right, qw[half_width:, :])
        pairs = matmul(left, kvw[:half_width, :]) + matmul(right, kvw[half_width:, :])
        cos = cosine[at, :]
        sin = sine[at, :]

        def rotary(u):
            turned = jnp.where(
                first_half,
                pltpu.roll(u, LANES - HEAD_SIZE // 2, 1),
                pltpu.roll(u, HEAD_SIZE // 2, 1),
            )
            return u * cos + turned * sin

        for pair in range(heads // 2):
            rot = rotary(queries[:, pair * LANES : (pair + 1) * LANES]).astype(jnp.bfloat16)
            rot = rot.astype(jnp.float32) * (1.0 / math.sqrt(HEAD_SIZE))
            even = jnp.where(key_lane, rot, 0.0)
            odd = jnp.where(key_lane, pltpu.roll(rot, HEAD_SIZE, 1), 0.0)
            qs[2 * pair, at, :] = even.astype(jnp.bfloat16)
            qs[2 * pair + 1, at, :] = odd.astype(jnp.bfloat16)
        entry = jnp.where(key_lane, rotary(pairs), pairs).astype(jnp.bfloat16)
        kv[pl.ds(WINDOW_LENGTH + step * PROJECT_ROWS, PROJECT_ROWS), :] = entry
        ents[0, at, :] = entry

    local[0].wait()
    local[1].wait()
    local[2].wait()
    tok_copy.wait_recv()
    project(0)

    local[4].wait()
    for copy in spread_copies:
        copy.wait_recv()
    own_rows = pl.ds(pl.multiple_of((tx * zn + me) * piece, piece), piece)
    gather_copies = []
    for e in range(zn):
        slot = slots[z_peer(e)]
        block = spread[lax.rem(me - slot + zn, zn)]
        if e == 0:
            kv[own_rows, :] = block
        else:
            stage[e] = block
            gather_copies.append(
                remote(stage.at[e], kv.at[own_rows], g_send.at[e], g_recv.at[e], {"dp": z_peer(e)})
            )
            gather_copies[-1].start()

    for step in range(1, rows // PROJECT_ROWS):
        project(step)

    for copy in gather_copies:
        copy.wait_recv()
    half = kv.at[pl.ds(pl.multiple_of(tx * half_rows, half_rows), half_rows)]
    half_copy = remote(half, half, half_sem.at[0], half_sem.at[1], sibling)
    half_copy.start()
    entry_copies = []
    for d in range(1, zn):
        entry_copies.append(
            remote(ents.at[0], ents.at[d], e_send.at[d], e_recv.at[d], {"dp": z_peer(d)})
        )
        entry_copies[-1].start()
    half_copy.wait_recv()

    stacked = heads * ROW_BLOCK
    chunks = kv.shape[0] // KEY_CHUNK
    old_chunks = WINDOW_LENGTH // KEY_CHUNK
    slices = KEY_CHUNK // LANES

    def att_copy(block, d):
        at = pl.ds(pl.multiple_of(block * ROW_BLOCK, ROW_BLOCK), ROW_BLOCK)
        return remote(
            att.at[0, at], att.at[d, at], a_send.at[block, d], a_recv.at[block, d], {"ty": y_peer(d)}
        )

    def attend(block, carry):
        start = pl.multiple_of(block * ROW_BLOCK, ROW_BLOCK)
        at = pl.ds(start, ROW_BLOCK)
        q = jnp.concatenate([qs[h, at, :] for h in range(heads)], axis=0)
        row = lax.rem(lax.broadcasted_iota(jnp.int32, (stacked, KEY_CHUNK), 0), ROW_BLOCK) + start
        column = lax.broadcasted_iota(jnp.int32, (1, KEY_CHUNK), 1)
        top = jnp.full((stacked, LANES), -jnp.inf, jnp.float32)
        for c in range(chunks):
            s = contract_last(q, kv[c * KEY_CHUNK : (c + 1) * KEY_CHUNK, :])
            if c < old_chunks:
                age = (offset - 1 - c * KEY_CHUNK - column) & (WINDOW_LENGTH - 1)
                last = jnp.where(age < length, WINDOW_LENGTH - 2 - age, -1)
                s = jnp.where(row <= last, s, -jnp.inf)
            else:
                s = jnp.where(row >= column + (c - old_chunks) * KEY_CHUNK, s, -jnp.inf)
            score[:, c * KEY_CHUNK : (c + 1) * KEY_CHUNK] = s
            for k in range(slices):
                top = jnp.maximum(top, s[:, k * LANES : (k + 1) * LANES])
        top = jnp.max(top, axis=1, keepdims=True)
        total = jnp.zeros((stacked, LANES), jnp.float32)
        summed = jnp.zeros((stacked, LANES), jnp.float32)
        for c in range(chunks):
            powers = jnp.exp(score[:, c * KEY_CHUNK : (c + 1) * KEY_CHUNK] - top)
            for k in range(slices):
                total = total + powers[:, k * LANES : (k + 1) * LANES]
            summed = summed + matmul(
                powers.astype(jnp.bfloat16), kv[c * KEY_CHUNK : (c + 1) * KEY_CHUNK, :]
            )
        result = summed / jnp.sum(total, axis=1, keepdims=True)
        low = lax.broadcasted_iota(jnp.int32, (ROW_BLOCK, LANES), 1) < HEAD_SIZE
        for pair in range(heads // 2):
            even = result[2 * pair * ROW_BLOCK : (2 * pair + 1) * ROW_BLOCK, :]
            odd = result[(2 * pair + 1) * ROW_BLOCK : (2 * pair + 2) * ROW_BLOCK, :]
            both = jnp.where(low, pltpu.roll(even, HEAD_SIZE, 1), odd)
            att[0, at, pair * LANES : (pair + 1) * LANES] = both.astype(jnp.bfloat16)
        for d in range(1, yn):
            att_copy(block, d).start()
        return carry

    lax.fori_loop(0, blocks, attend, 0)

    owner = jnp.int32(0)
    turn = jnp.int32(0)
    for r in range(zn):
        here = slots[r] == me
        owner = jnp.where(here, r, owner)
        turn = jnp.where(here, offsets[r], turn)
    for copy in entry_copies:
        copy.wait_recv()
    local[3].wait()
    entry = ents[lax.rem(me - owner + zn, zn)]
    target = lax.broadcasted_iota(jnp.int32, (KEY_CHUNK, rows), 1)
    for c in range(old_chunks):
        at = pl.ds(c * KEY_CHUNK, KEY_CHUNK)
        index = (lax.broadcasted_iota(jnp.int32, (KEY_CHUNK, rows), 0) + (c * KEY_CHUNK - turn)) & (
            WINDOW_LENGTH - 1
        )
        chosen = jnp.where(index == target, 1.0, 0.0).astype(jnp.bfloat16)
        written = matmul(chosen, entry)
        kept = old[at, :].astype(jnp.float32)
        new_cache[0, 0, at, :] = jnp.where(index[:, :LANES] < rows, written, kept).astype(jnp.bfloat16)

    for copy in w_copies:
        copy.wait_recv()
    local[5].wait()
    local[6].wait()
    part_copies = []
    for block in range(blocks):
        at = pl.ds(block * ROW_BLOCK, ROW_BLOCK)
        for d in range(1, yn):
            att_copy(block, d).wait_recv()
        pieces = [att[d, at, :] for d in range(yn)]
        other = matmul(pieces[0], wbuf[0, 1])
        for d in range(1, yn):
            other = other + matmul(pieces[d], wbuf[d, 1])
        psend[at, :] = other
        part_copies.append(
            remote(psend.at[at], precv.at[at], p_send.at[block], p_recv.at[block], sibling)
        )
        part_copies[-1].start()
        own = matmul(pieces[0], wbuf[0, 0])
        for d in range(1, yn):
            own = own + matmul(pieces[d], wbuf[d, 0])
        mine[at, :] = own
    for block in range(blocks):
        at = pl.ds(block * ROW_BLOCK, ROW_BLOCK)
        part_copies[block].wait_recv()
        mixed[at, :] = (mine[at, :] + precv[at, :]).astype(jnp.bfloat16)

    tok_copy.wait_send()
    half_copy.wait_send()
    for copy in spread_copies + w_copies + gather_copies + entry_copies + part_copies:
        copy.wait_send()
    for block in range(blocks):
        for d in range(1, yn):
            att_copy(block, d).wait_send()


def per_device(
    tokens, query_weight, key_value_weight, output_weight, cache, lengths, offsets, slots
):
    zn = lax.axis_size("dp")
    yn = lax.axis_size("ty")
    rows, half_width = tokens.shape
    width = 2 * half_width
    query_cols = query_weight.shape[2]
    heads = query_cols // HEAD_SIZE
    cols = width // (2 * yn)
    piece = WINDOW_LENGTH // (2 * zn)
    blocks = rows // ROW_BLOCK

    length = lengths[lax.axis_index("dp")]
    half_size = HEAD_SIZE // 2
    spot = jnp.arange(LANES, dtype=jnp.int32)
    freqs = jnp.exp(
        (spot % half_size).astype(jnp.float32) * (-2.0 * math.log(10000.0) / HEAD_SIZE)
    )
    positions = (length + jnp.arange(rows, dtype=jnp.int32)).astype(jnp.float32)
    angles = positions[:, None] * freqs[None, :]
    cosine = jnp.cos(angles)
    sine = jnp.where(spot[None, :] % HEAD_SIZE < half_size, -jnp.sin(angles), jnp.sin(angles))

    bf16 = jnp.bfloat16
    f32 = jnp.float32
    dma = pltpu.SemaphoreType.DMA
    anywhere = pl.BlockSpec(memory_space=pl.ANY)
    vmem = pl.BlockSpec(memory_space=pltpu.VMEM)
    smem = pl.BlockSpec(memory_space=pltpu.SMEM)
    flops = 2 * rows * (width * (query_cols + 2 * HEAD_SIZE + width // yn) + 4 * query_cols * (WINDOW_LENGTH + rows))
    return pl.pallas_call(
        functools.partial(kernel, zn, yn),
        out_shape=(
            jax.ShapeDtypeStruct((rows, cols), bf16),
            jax.ShapeDtypeStruct(cache.shape, bf16),
        ),
        in_specs=[anywhere] * 5 + [vmem] * 2 + [smem] * 3,
        out_specs=(vmem, vmem),
        scratch_shapes=[
            pltpu.VMEM((2, rows, half_width), bf16),
            pltpu.VMEM((width, query_cols), bf16),
            pltpu.VMEM((width, 2 * HEAD_SIZE), bf16),
            pltpu.VMEM((WINDOW_LENGTH, 2 * HEAD_SIZE), bf16),
            pltpu.VMEM((yn, 2, query_cols, cols), bf16),
            pltpu.VMEM((zn, piece, 2 * HEAD_SIZE), bf16),
            pltpu.VMEM((zn, piece, 2 * HEAD_SIZE), bf16),
            pltpu.VMEM((WINDOW_LENGTH + rows, 2 * HEAD_SIZE), bf16),
            pltpu.VMEM((zn, rows, 2 * HEAD_SIZE), bf16),
            pltpu.VMEM((heads, rows, LANES), bf16),
            pltpu.VMEM((yn, rows, query_cols), bf16),
            pltpu.VMEM((heads * ROW_BLOCK, WINDOW_LENGTH + rows), f32),
            pltpu.VMEM((rows, cols), f32),
            pltpu.VMEM((rows, cols), f32),
            pltpu.VMEM((rows, cols), f32),
            dma((7,)),
            dma((2,)),
            dma((yn, 2)),
            dma((yn, 2)),
            dma((zn,)),
            dma((zn,)),
            dma((zn,)),
            dma((zn,)),
            dma((2,)),
            dma((zn,)),
            dma((zn,)),
            dma((blocks, yn)),
            dma((blocks, yn)),
            dma((blocks,)),
            dma((blocks,)),
        ],
        compiler_params=pltpu.CompilerParams(
            collective_id=0, has_side_effects=True, vmem_limit_bytes=48 * 1024 * 1024
        ),
        cost_estimate=pl.CostEstimate(flops=flops, bytes_accessed=6 << 20, transcendentals=0),
    )(
        tokens,
        query_weight.reshape(width, query_cols),
        key_value_weight.reshape(width, 2 * HEAD_SIZE),
        output_weight,
        cache,
        cosine,
        sine,
        lengths,
        offsets,
        slots,
    )


def solution(mesh):
    return jax.shard_map(
        per_device,
        mesh=mesh,
        in_specs=(
            P("dp", "tx"),
            P(None, "ty", "tx"),
            P(None, "ty", None),
            P("ty", "tx", None),
            P("dp", "ty", None, None),
            P(),
            P(),
            P(),
        ),
        out_specs=(P("dp", ("tx", "ty")), P("dp", "ty", None, None)),
        check_vma=False,
    )
```

time: 145 us -> 53.2 us (0.37)
  the two profiles are of different devices: /device:TPU:0 before, /device:TPU:15 now
where the time goes in v1:
time: 53.2 us; the launch traced here: 52.9 us
  Pallas kernels  42.3 us (80%)
  local copies, waits for them, and re-layouts  8.17 us (15%)
  other arithmetic  1.67 us (3%)
  between operations  0.7 us (1%)
    pallas_call x1, Pallas kernels, per_device(): pl.pallas_call(functools.partial(kernel, zn, yn), out_shape=(jax.ShapeDty...  42.3 us
    unnamed x18, local copies, waits for them, and re-layouts  6.87 us
    dynamic_slice x1, local copies, waits for them, and re-layouts, per_device(): length = lengths[lax.axis_index('dp')]  1.3 us

profile of v1, /device:TPU:15, one launch (start us, length us, event | category | flops | bytes accessed | tf_op | source)
XLA Modules:
  0.0 52.9 jit_solution(608241504376543491)
XLA Ops:
  0.6 0.0 copy-start.3
  0.6 1.3 %dynamic_slice.3 = s32[1]{0:T(128)} dynamic-slice(s32[4]{0:T(128)} %lengths.1, s32[]{:T(128)S(6)} %select_n.29), dynamic_slice_sizes={1} | dynamic-slice | bytes 12 | tf_op jit(solution)/shard_map/dynamic_slice | solution.py:308
  2.0 0.7 %add_convert_fusion = f32[512]{0:T(512)S(1)} fusion(s32[]{:T(128)} %bitcast.2), kind=kLoop, calls=%fused_computation.3 | loop fusion | flops 1024 | bytes 2052 | tf_op jit(solution)/shard_map/convert_element_type | solution.py:314
  2.6 1.0 %negate_select_fusion = (f32[512,128]{1,0:T(8,128)S(1)}, f32[512,128]{1,0:T(8,128)S(1)}) fusion(f32[128]{0:T(128)S(1)} %fusion.2, f32[512]{0:T(512)S(1)} %add_convert_fusion, pred[128]{0:T(512)(128)(4,1)S(1)} %fusion.3), kind=kLoop, calls=%fused_computation | loop fusion | flops 196608 | bytes 526976 | tf_op jit(solution)/shard_map/jit(_where)/select_n | solution.py:317
  3.6 0.0 copy-start.5
  3.6 0.0 copy-start.6
  3.6 0.0 copy-start.7
  3.7 0.0 copy-done.3
  3.7 0.6 %copy-done.5 = s32[4]{0:T(128)S(1)} copy-done((s32[4]{0:T(128)S(1)}, s32[4]{0:T(128)}, u32[]{:S(2)}) %copy-start.5) | copy-done | bytes 40
  4.3 0.0 copy-done.6
  4.3 0.0 copy-done.7
  4.3 0.0 copy-start
  4.3 1.2 %copy-done = bf16[512,1024]{1,0:T(8,128)(2,1)S(1)} copy-done((bf16[512,1024]{1,0:T(8,128)(2,1)S(1)}, bf16[512,1024]{1,0:T(8,128)(2,1)}, u32[]{:S(2)}) %copy-start) | copy-done | bytes 1048600
  5.5 0.0 copy-start.1
  5.5 1.2 %copy-done.1 = bf16[2048,1,256]{2,0,1:T(8,128)(2,1)S(1)} copy-done((bf16[2048,1,256]{2,0,1:T(8,128)(2,1)S(1)}, bf16[2048,1,256]{2,0,1:T(8,128)(2,1)}, u32[]{:S(2)}) %copy-start.1) | copy-done | bytes 1048600
  6.8 0.0 copy-start.2
  6.8 1.2 %copy-done.2 = bf16[1,256,2048]{2,1,0:T(8,128)(2,1)S(1)} copy-done((bf16[1,256,2048]{2,1,0:T(8,128)(2,1)S(1)}, bf16[1,256,2048]{2,1,0:T(8,128)(2,1)}, u32[]{:S(2)}) %copy-start.2) | copy-done | bytes 1048600
  8.0 0.0 copy-start.4
  8.0 1.0 %copy-done.4 = bf16[1,1,2048,128]{3,2,1,0:T(8,128)(2,1)S(1)} copy-done((bf16[1,1,2048,128]{3,2,1,0:T(8,128)(2,1)S(1)}, bf16[1,1,2048,128]{3,2,1,0:T(8,128)(2,1)}, u32[]{:S(2)}) %copy-start.4) | copy-done | bytes 524312
  9.0 42.3 %shard_map.95 = (bf16[512,256]{1,0:T(8,128)(2,1)S(1)}, bf16[1,1,2048,128]{3,2,1,0:T(8,128)(2,1)S(1)}) custom-call(bf16[512,1024]{1,0:T(8,128)(2,1)S(1)} %copy-done, bf16[2048,256]{1,0:T(8,128)(2,1)S(1)} %bitcast.3, bf16[2048,128]{1,0:T(8,128)(2,1)S(1)} %bitcast.4, bf16[1,256,2048]{2,1,0:T(8,128)(2,1)S(1)} %copy-done.2, ...), custom_call_target="tpu_custom_call" | custom-call | flops 4563402752 | bytes 6291456 | tf_op jit(solution)/shard_map/pallas_call | solution.py:326
  51.4 0.7 %copy.12 = bf16[512,256]{1,0:T(8,128)(2,1)} copy(bf16[512,256]{1,0:T(8,128)(2,1)S(1)} %get-tuple-element.6) | data formatting | bytes 524288
  52.1 0.8 %copy.13 = bf16[1,1,2048,128]{3,2,1,0:T(8,128)(2,1)} copy(bf16[1,1,2048,128]{3,2,1,0:T(8,128)(2,1)S(1)} %get-tuple-element.7) | data formatting | bytes 1048576
  (2 shorter events, 0.0 us)
Async XLA Ops:
  0.6 3.0 %copy-start.3 = (bf16[2048,1,128]{2,0,1:T(8,128)(2,1)S(1)}, bf16[2048,1,128]{2,0,1:T(8,128)(2,1)}, u32[]{:S(2)}) copy-start(bf16[2048,1,128]{2,0,1:T(8,128)(2,1)} %param.10) | copy-start | bytes 1572868
  3.6 0.7 %copy-start.5 = (s32[4]{0:T(128)S(1)}, s32[4]{0:T(128)}, u32[]{:S(2)}) copy-start(s32[4]{0:T(128)} %lengths.1) | copy-start | bytes 52
  3.6 0.7 %copy-start.6 = (s32[4]{0:T(128)S(1)}, s32[4]{0:T(128)}, u32[]{:S(2)}) copy-start(s32[4]{0:T(128)} %offsets.1) | copy-start | bytes 52
  3.6 0.7 %copy-start.7 = (s32[4]{0:T(128)S(1)}, s32[4]{0:T(128)}, u32[]{:S(2)}) copy-start(s32[4]{0:T(128)} %slots.1) | copy-start | bytes 52
  4.3 1.2 %copy-start = (bf16[512,1024]{1,0:T(8,128)(2,1)S(1)}, bf16[512,1024]{1,0:T(8,128)(2,1)}, u32[]{:S(2)}) copy-start(bf16[512,1024]{1,0:T(8,128)(2,1)} %tokens.1) | copy-start | bytes 3145732
  5.5 1.2 %copy-start.1 = (bf16[2048,1,256]{2,0,1:T(8,128)(2,1)S(1)}, bf16[2048,1,256]{2,0,1:T(8,128)(2,1)}, u32[]{:S(2)}) copy-start(bf16[2048,1,256]{2,0,1:T(8,128)(2,1)} %param.9) | copy-start | bytes 3145732
  6.8 1.2 %copy-start.2 = (bf16[1,256,2048]{2,1,0:T(8,128)(2,1)S(1)}, bf16[1,256,2048]{2,1,0:T(8,128)(2,1)}, u32[]{:S(2)}) copy-start(bf16[1,256,2048]{2,1,0:T(8,128)(2,1)} %output_weight.1) | copy-start | bytes 3145732
  8.0 1.0 %copy-start.4 = (bf16[1,1,2048,128]{3,2,1,0:T(8,128)(2,1)S(1)}, bf16[1,1,2048,128]{3,2,1,0:T(8,128)(2,1)}, u32[]{:S(2)}) copy-start(bf16[1,1,2048,128]{3,2,1,0:T(8,128)(2,1)} %cache.1) | copy-start | bytes 1572868

commit v2 on v1

--- a/solution.py
+++ b/solution.py
@@ -34,10 +34,11 @@
 
 def kernel(
     zn, yn,
-    tokens, query_weight, key_value_weight, output_weight, cache, cosine, sine, lengths, offsets, slots,
+    tokens, query_weight, key_value_weight, output_weight, cache, lengths_in, offsets_in, slots_in,
     mixed, new_cache,
-    tok, qw, kvw, old, wbuf, spread, stage, kv, ents, qs, att, score, mine, psend, precv,
-    local_sem, tok_sem, w_send, w_recv, s_send, s_recv, g_send, g_recv, half_sem, e_send, e_recv,
+    lengths, offsets, slots, cosine, sine,
+    tok, qw, kvw, old, wbuf, spread, stage, kv, ents, qs, att, score, peak, mine, psend, precv,
+    local_sem, t_send, t_recv, w_send, w_recv, s_send, s_recv, g_send, g_recv, h_send, h_recv, e_send, e_recv,
     a_send, a_recv, p_send, p_recv,
 ):
     me = lax.axis_index("dp")
@@ -48,7 +49,6 @@
     cols = mixed.shape[1]
     heads = qs.shape[0]
     piece = spread.shape[1]
-    half_rows = zn * piece
     blocks = rows // ROW_BLOCK
     sibling = {"tx": 1 - tx}
 
@@ -75,7 +75,10 @@
 
     for side in range(2):
         local.append(pltpu.make_async_copy(w_columns(side, ty), wbuf.at[0, side], local_sem.at[5 + side]))
-    for copy in local:
+    local.append(pltpu.make_async_copy(lengths_in, lengths, local_sem.at[7]))
+    local.append(pltpu.make_async_copy(offsets_in, offsets, local_sem.at[8]))
+    local.append(pltpu.make_async_copy(slots_in, slots, local_sem.at[9]))
+    for copy in local[7:] + local[:7]:
         copy.start()
 
     barrier = pltpu.get_barrier_semaphore()
@@ -86,8 +89,14 @@
     pl.semaphore_signal(barrier, inc=1, device_id=sibling, device_id_type=MESH)
     pl.semaphore_wait(barrier, zn + yn - 1)
 
-    tok_copy = remote(tokens, tok.at[tx], tok_sem.at[0], tok_sem.at[1], sibling)
-    tok_copy.start()
+    steps = rows // PROJECT_ROWS
+    tok_copies = []
+    for step in range(steps):
+        at = pl.ds(step * PROJECT_ROWS, PROJECT_ROWS)
+        tok_copies.append(
+            remote(tokens.at[at], tok.at[tx, at], t_send.at[step], t_recv.at[step], sibling)
+        )
+        tok_copies[-1].start()
     spread_copies = []
     for d in range(1, zn):
         source = cache.at[0, 0, pl.ds(pl.multiple_of((tx * zn + z_peer(d)) * piece, piece), piece)]
@@ -106,8 +115,27 @@
             )
             w_copies[-1].start()
 
+    for copy in local[7:]:
+        copy.wait()
     length = lengths[me]
     offset = offsets[me]
+
+    spot = lax.broadcasted_iota(jnp.int32, (1, LANES), 1)
+    freqs = jnp.ones((1, LANES), jnp.float32)
+    for m in range(1, HEAD_SIZE // 2):
+        freqs = jnp.where(lax.rem(spot, HEAD_SIZE // 2) == m, 10000.0 ** (-2.0 * m / HEAD_SIZE), freqs)
+    sign = jnp.where(lax.rem(spot, HEAD_SIZE) < HEAD_SIZE // 2, -1.0, 1.0)
+
+    def tables(step, carry):
+        start = pl.multiple_of(step * ROW_BLOCK, ROW_BLOCK)
+        position = lax.broadcasted_iota(jnp.int32, (ROW_BLOCK, LANES), 0) + (length + start)
+        angles = position.astype(jnp.float32) * freqs
+        cosine[pl.ds(start, ROW_BLOCK), :] = jnp.cos(angles)
+        sine[pl.ds(start, ROW_BLOCK), :] = jnp.sin(angles) * sign
+        return carry
+
+    lax.fori_loop(0, blocks, tables, 0)
+
     lane = lax.broadcasted_iota(jnp.int32, (PROJECT_ROWS, LANES), 1)
     first_half = lax.rem(lane, HEAD_SIZE) < HEAD_SIZE // 2
     key_lane = lane < HEAD_SIZE
@@ -147,13 +175,17 @@
     local[0].wait()
     local[1].wait()
     local[2].wait()
-    tok_copy.wait_recv()
+    tok_copies[0].wait_recv()
     project(0)
 
     local[4].wait()
     for copy in spread_copies:
         copy.wait_recv()
-    own_rows = pl.ds(pl.multiple_of((tx * zn + me) * piece, piece), piece)
+    def window_rows(core, e):
+        quarter = lax.rem(me - e + zn, zn)
+        return pl.ds(pl.multiple_of((core * zn + quarter) * piece, piece), piece)
+
+    own_rows = window_rows(tx, 0)
     gather_copies = []
     for e in range(zn):
         slot = slots[z_peer(e)]
@@ -167,26 +199,82 @@
             )
             gather_copies[-1].start()
 
-    for step in range(1, rows // PROJECT_ROWS):
+    def forward(e):
+        here = kv.at[window_rows(tx, e)]
+        return remote(here, here, h_send.at[e], h_recv.at[e], sibling)
+
+    forward(0).start()
+    for step in range(1, steps):
+        tok_copies[step].wait_recv()
         project(step)
 
-    for copy in gather_copies:
-        copy.wait_recv()
-    half = kv.at[pl.ds(pl.multiple_of(tx * half_rows, half_rows), half_rows)]
-    half_copy = remote(half, half, half_sem.at[0], half_sem.at[1], sibling)
-    half_copy.start()
+    stacked = heads * ROW_BLOCK
+    chunks = kv.shape[0] // KEY_CHUNK
+    old_chunks = WINDOW_LENGTH // KEY_CHUNK
+    slices = KEY_CHUNK // LANES
+    part = KEY_CHUNK // 2
+    by_piece = piece == part
+
+    def bases(c):
+        if by_piece:
+            quarter = lax.rem(me - c + zn, zn)
+            return [pl.multiple_of((core * zn + quarter) * part, part) for core in range(2)]
+        return [c * KEY_CHUNK, c * KEY_CHUNK + part]
+
+    def chunk_rows(c):
+        if c >= old_chunks:
+            return kv[c * KEY_CHUNK : (c + 1) * KEY_CHUNK, :]
+        return jnp.concatenate([kv[pl.ds(base, part), :] for base in bases(c)], axis=0)
+
+    def score_chunk(c, first):
+        def one(block, carry):
+            start = pl.multiple_of(block * ROW_BLOCK, ROW_BLOCK)
+            q = jnp.concatenate([qs[h, pl.ds(start, ROW_BLOCK), :] for h in range(heads)], axis=0)
+            row = lax.rem(lax.broadcasted_iota(jnp.int32, (stacked, KEY_CHUNK), 0), ROW_BLOCK) + start
+            column = lax.broadcasted_iota(jnp.int32, (1, KEY_CHUNK), 1)
+            s = contract_last(q, chunk_rows(c))
+            if c < old_chunks:
+                low, high = bases(c)
+                cycle = jnp.where(column < part, column + low, column + (high - part))
+                age = (offset - 1 - cycle) & (WINDOW_LENGTH - 1)
+                last = jnp.where(age < length, WINDOW_LENGTH - 2 - age, -1)
+                s = jnp.where(row <= last, s, -jnp.inf)
+            else:
+                s = jnp.where(row >= column + (c - old_chunks) * KEY_CHUNK, s, -jnp.inf)
+            score[block, :, c * KEY_CHUNK : (c + 1) * KEY_CHUNK] = s
+            top = s[:, :LANES]
+            for k in range(1, slices):
+                top = jnp.maximum(top, s[:, k * LANES : (k + 1) * LANES])
+            if not first:
+                top = jnp.maximum(top, peak[block])
+            peak[block] = top
+            return carry
+
+        lax.fori_loop(0, blocks, one, 0)
+
+    for c in range(old_chunks, chunks):
+        score_chunk(c, c == old_chunks)
+
     entry_copies = []
     for d in range(1, zn):
         entry_copies.append(
             remote(ents.at[0], ents.at[d], e_send.at[d], e_recv.at[d], {"dp": z_peer(d)})
         )
-        entry_copies[-1].start()
-    half_copy.wait_recv()
-
-    stacked = heads * ROW_BLOCK
-    chunks = kv.shape[0] // KEY_CHUNK
-    old_chunks = WINDOW_LENGTH // KEY_CHUNK
-    slices = KEY_CHUNK // LANES
+    order = [0, 1, 3, 2] if by_piece else list(range(zn))
+    for spot_in_order, e in enumerate(order):
+        if spot_in_order + 1 < zn:
+            later = order[spot_in_order + 1]
+            gather_copies[later - 1].wait_recv()
+            forward(later).start()
+        else:
+            for copy in entry_copies:
+                copy.start()
+        forward(e).wait_recv()
+        if by_piece:
+            score_chunk(e, False)
+    if not by_piece:
+        for c in range(old_chunks):
+            score_chunk(c, False)
 
     def att_copy(block, d):
         at = pl.ds(pl.multiple_of(block * ROW_BLOCK, ROW_BLOCK), ROW_BLOCK)
@@ -197,31 +285,14 @@
     def attend(block, carry):
         start = pl.multiple_of(block * ROW_BLOCK, ROW_BLOCK)
         at = pl.ds(start, ROW_BLOCK)
-        q = jnp.concatenate([qs[h, at, :] for h in range(heads)], axis=0)
-        row = lax.rem(lax.broadcasted_iota(jnp.int32, (stacked, KEY_CHUNK), 0), ROW_BLOCK) + start
-        column = lax.broadcasted_iota(jnp.int32, (1, KEY_CHUNK), 1)
-        top = jnp.full((stacked, LANES), -jnp.inf, jnp.float32)
-        for c in range(chunks):
-            s = contract_last(q, kv[c * KEY_CHUNK : (c + 1) * KEY_CHUNK, :])
-            if c < old_chunks:
-                age = (offset - 1 - c * KEY_CHUNK - column) & (WINDOW_LENGTH - 1)
-                last = jnp.where(age < length, WINDOW_LENGTH - 2 - age, -1)
-                s = jnp.where(row <= last, s, -jnp.inf)
-            else:
-                s = jnp.where(row >= column + (c - old_chunks) * KEY_CHUNK, s, -jnp.inf)
-            score[:, c * KEY_CHUNK : (c + 1) * KEY_CHUNK] = s
-            for k in range(slices):
-                top = jnp.maximum(top, s[:, k * LANES : (k + 1) * LANES])
-        top = jnp.max(top, axis=1, keepdims=True)
+        top = jnp.max(peak[block], axis=1, keepdims=True)
         total = jnp.zeros((stacked, LANES), jnp.float32)
         summed = jnp.zeros((stacked, LANES), jnp.float32)
         for c in range(chunks):
-            powers = jnp.exp(score[:, c * KEY_CHUNK : (c + 1) * KEY_CHUNK] - top)
+            powers = jnp.exp(score[block, :, c * KEY_CHUNK : (c + 1) * KEY_CHUNK] - top)
             for k in range(slices):
                 total = total + powers[:, k * LANES : (k + 1) * LANES]
-            summed = summed + matmul(
-                powers.astype(jnp.bfloat16), kv[c * KEY_CHUNK : (c + 1) * KEY_CHUNK, :]
-            )
+            summed = summed + matmul(powers.astype(jnp.bfloat16), chunk_rows(c))
         result = summed / jnp.sum(total, axis=1, keepdims=True)
         low = lax.broadcasted_iota(jnp.int32, (ROW_BLOCK, LANES), 1) < HEAD_SIZE
         for pair in range(heads // 2):
@@ -283,9 +354,9 @@
         part_copies[block].wait_recv()
         mixed[at, :] = (mine[at, :] + precv[at, :]).astype(jnp.bfloat16)
 
-    tok_copy.wait_send()
-    half_copy.wait_send()
-    for copy in spread_copies + w_copies + gather_copies + entry_copies + part_copies:
+    for e in range(zn):
+        forward(e).wait_send()
+    for copy in tok_copies + spread_copies + w_copies + gather_copies + entry_copies + part_copies:
         copy.wait_send()
     for block in range(blocks):
         for d in range(1, yn):
@@ -305,23 +376,11 @@
     piece = WINDOW_LENGTH // (2 * zn)
     blocks = rows // ROW_BLOCK
 
-    length = lengths[lax.axis_index("dp")]
-    half_size = HEAD_SIZE // 2
-    spot = jnp.arange(LANES, dtype=jnp.int32)
-    freqs = jnp.exp(
-        (spot % half_size).astype(jnp.float32) * (-2.0 * math.log(10000.0) / HEAD_SIZE)
-    )
-    positions = (length + jnp.arange(rows, dtype=jnp.int32)).astype(jnp.float32)
-    angles = positions[:, None] * freqs[None, :]
-    cosine = jnp.cos(angles)
-    sine = jnp.where(spot[None, :] % HEAD_SIZE < half_size, -jnp.sin(angles), jnp.sin(angles))
-
     bf16 = jnp.bfloat16
     f32 = jnp.float32
     dma = pltpu.SemaphoreType.DMA
-    anywhere = pl.BlockSpec(memory_space=pl.ANY)
+    hbm = pl.BlockSpec(memory_space=pltpu.HBM)
     vmem = pl.BlockSpec(memory_space=pltpu.VMEM)
-    smem = pl.BlockSpec(memory_space=pltpu.SMEM)
     flops = 2 * rows * (width * (query_cols + 2 * HEAD_SIZE + width // yn) + 4 * query_cols * (WINDOW_LENGTH + rows))
     return pl.pallas_call(
         functools.partial(kernel, zn, yn),
@@ -329,9 +388,14 @@
             jax.ShapeDtypeStruct((rows, cols), bf16),
             jax.ShapeDtypeStruct(cache.shape, bf16),
         ),
-        in_specs=[anywhere] * 5 + [vmem] * 2 + [smem] * 3,
+        in_specs=[hbm] * 8,
         out_specs=(vmem, vmem),
         scratch_shapes=[
+            pltpu.SMEM(lengths.shape, jnp.int32),
+            pltpu.SMEM(offsets.shape, jnp.int32),
+            pltpu.SMEM(slots.shape, jnp.int32),
+            pltpu.VMEM((rows, LANES), f32),
+            pltpu.VMEM((rows, LANES), f32),
             pltpu.VMEM((2, rows, half_width), bf16),
             pltpu.VMEM((width, query_cols), bf16),
             pltpu.VMEM((width, 2 * HEAD_SIZE), bf16),
@@ -343,19 +407,22 @@
             pltpu.VMEM((zn, rows, 2 * HEAD_SIZE), bf16),
             pltpu.VMEM((heads, rows, LANES), bf16),
             pltpu.VMEM((yn, rows, query_cols), bf16),
-            pltpu.VMEM((heads * ROW_BLOCK, WINDOW_LENGTH + rows), f32),
+            pltpu.VMEM((blocks, heads * ROW_BLOCK, WINDOW_LENGTH + rows), f32),
+            pltpu.VMEM((blocks, heads * ROW_BLOCK, LANES), f32),
             pltpu.VMEM((rows, cols), f32),
             pltpu.VMEM((rows, cols), f32),
             pltpu.VMEM((rows, cols), f32),
-            dma((7,)),
-            dma((2,)),
+            dma((10,)),
+            dma((rows // PROJECT_ROWS,)),
+            dma((rows // PROJECT_ROWS,)),
             dma((yn, 2)),
             dma((yn, 2)),
             dma((zn,)),
             dma((zn,)),
             dma((zn,)),
             dma((zn,)),
-            dma((2,)),
+            dma((zn,)),
+            dma((zn,)),
             dma((zn,)),
             dma((zn,)),
             dma((blocks, yn)),
@@ -364,7 +431,7 @@
             dma((blocks,)),
         ],
         compiler_params=pltpu.CompilerParams(
-            collective_id=0, has_side_effects=True, vmem_limit_bytes=48 * 1024 * 1024
+            collective_id=0, has_side_effects=True, vmem_limit_bytes=46 * 1024 * 1024
         ),
         cost_estimate=pl.CostEstimate(flops=flops, bytes_accessed=6 << 20, transcendentals=0),
     )(
@@ -373,8 +440,6 @@
         key_value_weight.reshape(width, 2 * HEAD_SIZE),
         output_weight,
         cache,
-        cosine,
-        sine,
         lengths,
         offsets,
         slots,

time: 53.2 us -> 48.1 us (0.904)
  the two profiles are of different devices: /device:TPU:15 before, /device:TPU:0 now
where the time goes in v2:
time: 48.1 us; the launch traced here: 47.8 us
  Pallas kernels  39.2 us (81%)
  local copies, waits for them, and re-layouts  7.92 us (16%)
  between operations  0.67 us (1%)
    pallas_call x1, Pallas kernels, per_device(): pl.pallas_call(functools.partial(kernel, zn, yn), out_shape=(jax.ShapeDty...  39.2 us
    unnamed x18, local copies, waits for them, and re-layouts  7.92 us

profile of v2, /device:TPU:0, one launch (start us, length us, event | category | flops | bytes accessed | tf_op | source)
XLA Modules:
  0.0 47.8 jit_solution(11133239739656865651)
XLA Ops:
  0.6 0.0 copy-start.5
  0.6 0.0 copy-start.6
  0.7 0.0 copy-start.7
  0.7 0.6 %copy-done.5 = s32[4]{0:T(128)S(1)} copy-done((s32[4]{0:T(128)S(1)}, s32[4]{0:T(128)}, u32[]{:S(2)}) %copy-start.5) | copy-done | bytes 40
  1.3 0.0 copy-done.6
  1.3 0.0 copy-done.7
  1.3 0.0 copy-start
  1.3 1.2 %copy-done = bf16[512,1024]{1,0:T(8,128)(2,1)S(1)} copy-done((bf16[512,1024]{1,0:T(8,128)(2,1)S(1)}, bf16[512,1024]{1,0:T(8,128)(2,1)}, u32[]{:S(2)}) %copy-start) | copy-done | bytes 1048600
  2.5 0.0 copy-start.1
  2.5 1.2 %copy-done.1 = bf16[2048,1,256]{2,0,1:T(8,128)(2,1)S(1)} copy-done((bf16[2048,1,256]{2,0,1:T(8,128)(2,1)S(1)}, bf16[2048,1,256]{2,0,1:T(8,128)(2,1)}, u32[]{:S(2)}) %copy-start.1) | copy-done | bytes 1048600
  3.8 0.0 copy-start.2
  3.8 1.2 %copy-done.2 = bf16[1,256,2048]{2,1,0:T(8,128)(2,1)S(1)} copy-done((bf16[1,256,2048]{2,1,0:T(8,128)(2,1)S(1)}, bf16[1,256,2048]{2,1,0:T(8,128)(2,1)}, u32[]{:S(2)}) %copy-start.2) | copy-done | bytes 1048600
  5.0 0.0 copy-start.3
  5.0 1.0 %copy-done.3 = bf16[2048,1,128]{2,0,1:T(8,128)(2,1)S(1)} copy-done((bf16[2048,1,128]{2,0,1:T(8,128)(2,1)S(1)}, bf16[2048,1,128]{2,0,1:T(8,128)(2,1)}, u32[]{:S(2)}) %copy-start.3) | copy-done | bytes 524312
  6.0 0.0 copy-start.4
  6.0 1.0 %copy-done.4 = bf16[1,1,2048,128]{3,2,1,0:T(8,128)(2,1)S(1)} copy-done((bf16[1,1,2048,128]{3,2,1,0:T(8,128)(2,1)S(1)}, bf16[1,1,2048,128]{3,2,1,0:T(8,128)(2,1)}, u32[]{:S(2)}) %copy-start.4) | copy-done | bytes 524312
  7.1 39.2 %shard_map.95 = (bf16[512,256]{1,0:T(8,128)(2,1)S(1)}, bf16[1,1,2048,128]{3,2,1,0:T(8,128)(2,1)S(1)}) custom-call(bf16[512,1024]{1,0:T(8,128)(2,1)S(1)} %copy-done, bf16[2048,256]{1,0:T(8,128)(2,1)S(1)} %bitcast.2, bf16[2048,128]{1,0:T(8,128)(2,1)S(1)} %bitcast.3, bf16[1,256,2048]{2,1,0:T(8,128)(2,1)S(1)} %copy-done.2, ...), custom_call_target="tpu_custom_call" | custom-call | flops 4563402752 | bytes 6291456 | tf_op jit(solution)/shard_map/pallas_call | solution.py:385
  46.3 0.7 %copy.12 = bf16[512,256]{1,0:T(8,128)(2,1)} copy(bf16[512,256]{1,0:T(8,128)(2,1)S(1)} %get-tuple-element.4) | data formatting | bytes 524288
  47.0 0.8 %copy.13 = bf16[1,1,2048,128]{3,2,1,0:T(8,128)(2,1)} copy(bf16[1,1,2048,128]{3,2,1,0:T(8,128)(2,1)S(1)} %get-tuple-element.5) | data formatting | bytes 1048576
Async XLA Ops:
  0.6 0.7 %copy-start.5 = (s32[4]{0:T(128)S(1)}, s32[4]{0:T(128)}, u32[]{:S(2)}) copy-start(s32[4]{0:T(128)} %lengths_in.1) | copy-start | bytes 52
  0.6 0.7 %copy-start.6 = (s32[4]{0:T(128)S(1)}, s32[4]{0:T(128)}, u32[]{:S(2)}) copy-start(s32[4]{0:T(128)} %offsets_in.1) | copy-start | bytes 52
  0.7 0.7 %copy-start.7 = (s32[4]{0:T(128)S(1)}, s32[4]{0:T(128)}, u32[]{:S(2)}) copy-start(s32[4]{0:T(128)} %slots_in.1) | copy-start | bytes 52
  1.3 1.2 %copy-start = (bf16[512,1024]{1,0:T(8,128)(2,1)S(1)}, bf16[512,1024]{1,0:T(8,128)(2,1)}, u32[]{:S(2)}) copy-start(bf16[512,1024]{1,0:T(8,128)(2,1)} %tokens.1) | copy-start | bytes 3145732
  2.5 1.2 %copy-start.1 = (bf16[2048,1,256]{2,0,1:T(8,128)(2,1)S(1)}, bf16[2048,1,256]{2,0,1:T(8,128)(2,1)}, u32[]{:S(2)}) copy-start(bf16[2048,1,256]{2,0,1:T(8,128)(2,1)} %param.9) | copy-start | bytes 3145732
  3.8 1.2 %copy-start.2 = (bf16[1,256,2048]{2,1,0:T(8,128)(2,1)S(1)}, bf16[1,256,2048]{2,1,0:T(8,128)(2,1)}, u32[]{:S(2)}) copy-start(bf16[1,256,2048]{2,1,0:T(8,128)(2,1)} %output_weight.1) | copy-start | bytes 3145732
  5.0 1.0 %copy-start.3 = (bf16[2048,1,128]{2,0,1:T(8,128)(2,1)S(1)}, bf16[2048,1,128]{2,0,1:T(8,128)(2,1)}, u32[]{:S(2)}) copy-start(bf16[2048,1,128]{2,0,1:T(8,128)(2,1)} %param.10) | copy-start | bytes 1572868
  6.0 1.0 %copy-start.4 = (bf16[1,1,2048,128]{3,2,1,0:T(8,128)(2,1)S(1)}, bf16[1,1,2048,128]{3,2,1,0:T(8,128)(2,1)}, u32[]{:S(2)}) copy-start(bf16[1,1,2048,128]{3,2,1,0:T(8,128)(2,1)} %cache.1) | copy-start | bytes 1572868

commit v3 on v2

--- a/solution.py
+++ b/solution.py
@@ -230,24 +230,27 @@
         def one(block, carry):
             start = pl.multiple_of(block * ROW_BLOCK, ROW_BLOCK)
             q = jnp.concatenate([qs[h, pl.ds(start, ROW_BLOCK), :] for h in range(heads)], axis=0)
-            row = lax.rem(lax.broadcasted_iota(jnp.int32, (stacked, KEY_CHUNK), 0), ROW_BLOCK) + start
+            row = lax.broadcasted_iota(jnp.int32, (ROW_BLOCK, KEY_CHUNK), 0) + start
             column = lax.broadcasted_iota(jnp.int32, (1, KEY_CHUNK), 1)
-            s = contract_last(q, chunk_rows(c))
             if c < old_chunks:
                 low, high = bases(c)
                 cycle = jnp.where(column < part, column + low, column + (high - part))
                 age = (offset - 1 - cycle) & (WINDOW_LENGTH - 1)
                 last = jnp.where(age < length, WINDOW_LENGTH - 2 - age, -1)
-                s = jnp.where(row <= last, s, -jnp.inf)
+                bias = jnp.where(row <= last, 0.0, -jnp.inf)
             else:
-                s = jnp.where(row >= column + (c - old_chunks) * KEY_CHUNK, s, -jnp.inf)
-            score[block, :, c * KEY_CHUNK : (c + 1) * KEY_CHUNK] = s
-            top = s[:, :LANES]
-            for k in range(1, slices):
-                top = jnp.maximum(top, s[:, k * LANES : (k + 1) * LANES])
-            if not first:
-                top = jnp.maximum(top, peak[block])
-            peak[block] = top
+                bias = jnp.where(row >= column + (c - old_chunks) * KEY_CHUNK, 0.0, -jnp.inf)
+            s = contract_last(q, chunk_rows(c))
+            for h in range(heads):
+                at = pl.ds(h * ROW_BLOCK, ROW_BLOCK)
+                mine_s = s[h * ROW_BLOCK : (h + 1) * ROW_BLOCK, :] + bias
+                score[block, at, c * KEY_CHUNK : (c + 1) * KEY_CHUNK] = mine_s
+                top = mine_s[:, :LANES]
+                for k in range(1, slices):
+                    top = jnp.maximum(top, mine_s[:, k * LANES : (k + 1) * LANES])
+                if not first:
+                    top = jnp.maximum(top, peak[block, at, :])
+                peak[block, at, :] = top
             return carry
 
         lax.fori_loop(0, blocks, one, 0)
@@ -431,7 +434,7 @@
             dma((blocks,)),
         ],
         compiler_params=pltpu.CompilerParams(
-            collective_id=0, has_side_effects=True, vmem_limit_bytes=46 * 1024 * 1024
+            collective_id=0, has_side_effects=True, vmem_limit_bytes=56 * 1024 * 1024
         ),
         cost_estimate=pl.CostEstimate(flops=flops, bytes_accessed=6 << 20, transcendentals=0),
     )(

time: 48.1 us -> 43.3 us (0.900)
  local copies, waits for them, and re-layouts: 7.92 us -> 2.52 us
  Pallas kernels: 39.2 us -> 40 us
    unnamed x18 -> x4, local copies, waits for them, and re-layouts: 7.92 us -> 2.52 us
    pallas_call x1, Pallas kernels: 39.2 us -> 40 us  [per_device(): pl.pallas_call(functools.partial(kernel, zn, yn), out_shape=(jax.ShapeDty...]
where the time goes in v3:
time: 43.3 us; the launch traced here: 43.2 us
  Pallas kernels  40 us (92%)
  local copies, waits for them, and re-layouts  2.52 us (6%)
  between operations  0.65 us (2%)
    pallas_call x1, Pallas kernels, per_device(): pl.pallas_call(functools.partial(kernel, zn, yn), out_shape=(jax.ShapeDty...  40 us
    unnamed x4, local copies, waits for them, and re-layouts  2.52 us

profile of v3, /device:TPU:0, one launch (start us, length us, event | category | flops | bytes accessed | tf_op | source)
XLA Modules:
  0.0 43.2 jit_solution(7597245514600364206)
XLA Ops:
  0.6 40.0 %shard_map.95 = (bf16[512,256]{1,0:T(8,128)(2,1)}, bf16[1,1,2048,128]{3,2,1,0:T(8,128)(2,1)}) custom-call(bf16[512,1024]{1,0:T(8,128)(2,1)} %tokens.1, bf16[2048,256]{1,0:T(8,128)(2,1)} %bitcast.2, bf16[2048,128]{1,0:T(8,128)(2,1)} %bitcast.3, bf16[1,256,2048]{2,1,0:T(8,128)(2,1)} %output_weight.1, bf16[1,1,2048,128]{3,2,1,0:T(8,128)(2,1)} %cache.1, ...), custom_call_target="tpu_custom_call" | custom-call | flops 4563402752 | bytes 6291456 | tf_op jit(solution)/shard_map/pallas_call | solution.py:388
  40.6 0.0 copy-start
  40.6 1.7 %copy.12 = bf16[512,256]{1,0:T(8,128)(2,1)} copy(bf16[512,256]{1,0:T(8,128)(2,1)} %get-tuple-element.4) | data formatting | bytes 524288
  42.4 0.0 copy-done
  42.4 0.8 %copy.13 = bf16[1,1,2048,128]{3,2,1,0:T(8,128)(2,1)} copy(bf16[1,1,2048,128]{3,2,1,0:T(8,128)(2,1)S(1)} %copy-done) | data formatting | bytes 1048576
Async XLA Ops:
  40.6 1.7 %copy-start = (bf16[1,1,2048,128]{3,2,1,0:T(8,128)(2,1)S(1)}, bf16[1,1,2048,128]{3,2,1,0:T(8,128)(2,1)}, u32[]{:S(2)}) copy-start(bf16[1,1,2048,128]{3,2,1,0:T(8,128)(2,1)} %get-tuple-element.5) | copy-start | bytes 1572868

commit v4 on v3

--- a/solution.py
+++ b/solution.py
@@ -226,7 +226,7 @@
             return kv[c * KEY_CHUNK : (c + 1) * KEY_CHUNK, :]
         return jnp.concatenate([kv[pl.ds(base, part), :] for base in bases(c)], axis=0)
 
-    def score_chunk(c, first):
+    def score_block(c, first):
         def one(block, carry):
             start = pl.multiple_of(block * ROW_BLOCK, ROW_BLOCK)
             q = jnp.concatenate([qs[h, pl.ds(start, ROW_BLOCK), :] for h in range(heads)], axis=0)
@@ -253,7 +253,10 @@
                 peak[block, at, :] = top
             return carry
 
-        lax.fori_loop(0, blocks, one, 0)
+        return one
+
+    def score_chunk(c, first):
+        lax.fori_loop(0, blocks, score_block(c, first), 0)
 
     for c in range(old_chunks, chunks):
         score_chunk(c, c == old_chunks)
@@ -273,10 +276,11 @@
             for copy in entry_copies:
                 copy.start()
         forward(e).wait_recv()
-        if by_piece:
+        if by_piece and spot_in_order + 1 < zn:
             score_chunk(e, False)
+    final_chunk = order[-1] if by_piece else old_chunks - 1
     if not by_piece:
-        for c in range(old_chunks):
+        for c in range(old_chunks - 1):
             score_chunk(c, False)
 
     def att_copy(block, d):
@@ -288,6 +292,7 @@
     def attend(block, carry):
         start = pl.multiple_of(block * ROW_BLOCK, ROW_BLOCK)
         at = pl.ds(start, ROW_BLOCK)
+        score_block(final_chunk, False)(block, carry)
         top = jnp.max(peak[block], axis=1, keepdims=True)
         total = jnp.zeros((stacked, LANES), jnp.float32)
         summed = jnp.zeros((stacked, LANES), jnp.float32)

time: 43.3 us -> 42.5 us (0.982)
  Pallas kernels: 40 us -> 39.1 us
    pallas_call x1, Pallas kernels: 40 us -> 39.1 us  [per_device(): pl.pallas_call(functools.partial(kernel, zn, yn), out_shape=(jax.ShapeDty...]
where the time goes in v4:
time: 42.5 us; the launch traced here: 42.3 us
  Pallas kernels  39.1 us (92%)
  local copies, waits for them, and re-layouts  2.52 us (6%)
  between operations  0.65 us (2%)
    pallas_call x1, Pallas kernels, per_device(): pl.pallas_call(functools.partial(kernel, zn, yn), out_shape=(jax.ShapeDty...  39.1 us
    unnamed x4, local copies, waits for them, and re-layouts  2.52 us

profile of v4, /device:TPU:0, one launch (start us, length us, event | category | flops | bytes accessed | tf_op | source)
XLA Modules:
  0.0 42.3 jit_solution(18361412177792614938)
XLA Ops:
  0.6 39.1 %shard_map.95 = (bf16[512,256]{1,0:T(8,128)(2,1)}, bf16[1,1,2048,128]{3,2,1,0:T(8,128)(2,1)}) custom-call(bf16[512,1024]{1,0:T(8,128)(2,1)} %tokens.1, bf16[2048,256]{1,0:T(8,128)(2,1)} %bitcast.2, bf16[2048,128]{1,0:T(8,128)(2,1)} %bitcast.3, bf16[1,256,2048]{2,1,0:T(8,128)(2,1)} %output_weight.1, bf16[1,1,2048,128]{3,2,1,0:T(8,128)(2,1)} %cache.1, ...), custom_call_target="tpu_custom_call" | custom-call | flops 4563402752 | bytes 6291456 | tf_op jit(solution)/shard_map/pallas_call | solution.py:393
  39.8 0.0 copy-start
  39.8 1.7 %copy.12 = bf16[512,256]{1,0:T(8,128)(2,1)} copy(bf16[512,256]{1,0:T(8,128)(2,1)} %get-tuple-element.4) | data formatting | bytes 524288
  41.5 0.0 copy-done
  41.5 0.8 %copy.13 = bf16[1,1,2048,128]{3,2,1,0:T(8,128)(2,1)} copy(bf16[1,1,2048,128]{3,2,1,0:T(8,128)(2,1)S(1)} %copy-done) | data formatting | bytes 1048576
Async XLA Ops:
  39.8 1.7 %copy-start = (bf16[1,1,2048,128]{3,2,1,0:T(8,128)(2,1)S(1)}, bf16[1,1,2048,128]{3,2,1,0:T(8,128)(2,1)}, u32[]{:S(2)}) copy-start(bf16[1,1,2048,128]{3,2,1,0:T(8,128)(2,1)} %get-tuple-element.5) | copy-start | bytes 1572868
